TPU v7x, 256 devices: a whole 4x4x8 slice. The times are simulated.
256 devices in a mesh: dp: 8 (over y, x_hi), shard: 32 (over x_lo, z, core).
Axes of the slice: x: 4 (x_hi: 2, x_lo: 2; x = x_hi * 2 + x_lo), y: 4, z: 8, core: 2. Of those that a mesh axis runs over, the one named last changes fastest.
Arguments:
- tokens: bfloat16 [8192, 2560], P('dp'), may hold values from -6 to 6
- masters: float32 [8, 1600, 5120], P('dp', 'shard'), may hold values from -0.125 to 0.125
- cotangent: bfloat16 [8192, 12800], P('dp', 'shard'), may hold values from -6 to 6
- partner: int32 [31, 32], replicated, may hold values from 0 to 31, as said below
- slots: int32 [31, 32], replicated, may hold values from 0 to 49, as said below
Outputs:
- masters_new: float32 [8, 1600, 5120], P('dp', 'shard')
- hidden: bfloat16 [8192, 12800], P('dp', 'shard')
- input_grad: bfloat16 [8192, 2560], P(('dp', 'shard'))
- master_grads: float32 [8, 1600, 5120], P('dp', 'shard')
Inputs may be any that keep to these rules, and one draw needn't show every extreme that they name: In every round partner is an involution without fixed points: partner[r, partner[r, s]] = s and partner[r, s] != s. Over the 31 rounds every shard index meets every other exactly once. The 31 slots of one shard index are distinct.
All inputs are finite; a program needn't handle non-finite values.
Results may differ from a plain program's by a relative error of at most 0.0066.
Values may be sent and summed in bfloat16 or wider, within the bound.
A program may use at most 192 MiB of HBM per device.

v0:
```python
import math

import jax
import jax.numpy as jnp
from jax import lax
from jax.sharding import PartitionSpec as P

exact = lax.Precision.HIGHEST


def body(tokens, masters, cotangent, partner, slots):
    width = tokens.shape[1]
    pages = masters.shape[1]
    shards = lax.axis_size("shard")
    groups = lax.axis_size("dp")
    member = lax.axis_index("shard")
    local = masters[0]
    my_partner = lax.dynamic_index_in_dim(partner, member, 1, False)
    my_slot = lax.dynamic_index_in_dim(slots, member, 1, False)
    to_peer = (my_partner[:, None] == jnp.arange(shards, dtype=jnp.int32)[None, :]).astype(
        jnp.float32
    )
    at_slot = (my_slot[:, None] == jnp.arange(pages, dtype=jnp.int32)[None, :]).astype(jnp.float32)
    picker = jnp.dot(to_peer.T, at_slot, precision=exact)
    outgoing = jnp.dot(picker, local, precision=exact)
    incoming = lax.all_to_all(outgoing, "shard", split_axis=0, concat_axis=0, tiled=True)
    kept = 1.0 - jnp.sum(picker, axis=0)
    renewed = local * kept[:, None] + jnp.dot(picker.T, incoming, precision=exact)
    wide = lax.all_gather(renewed.astype(jnp.bfloat16), "dp", axis=0, tiled=True)
    gate_w = wide[:, :width]
    up_w = wide[:, width:]
    gate = jnp.einsum("td,hd->th", tokens, gate_w, preferred_element_type=jnp.float32)
    up = jnp.einsum("td,hd->th", tokens, up_w, preferred_element_type=jnp.float32)
    sig = jax.nn.sigmoid(gate)
    active = gate * sig
    hidden = (active * up).astype(jnp.bfloat16)
    grad_in = cotangent.astype(jnp.float32)
    d_gate = (grad_in * up * sig * (1.0 + gate * (1.0 - sig))).astype(jnp.bfloat16)
    d_up = (grad_in * active).astype(jnp.bfloat16)
    input_grad = lax.psum_scatter(
        jnp.dot(d_gate, gate_w, preferred_element_type=jnp.float32)
        + jnp.dot(d_up, up_w, preferred_element_type=jnp.float32),
        "shard",
        scatter_dimension=0,
        tiled=True,
    ).astype(jnp.bfloat16)
    summed = lax.psum_scatter(
        jnp.concatenate(
            (
                jnp.einsum("th,td->hd", d_gate, tokens, preferred_element_type=jnp.float32),
                jnp.einsum("th,td->hd", d_up, tokens, preferred_element_type=jnp.float32),
            ),
            axis=1,
        ),
        "dp",
        scatter_dimension=0,
        tiled=True,
    )
    scaled = summed * (1.0 / math.sqrt(tokens.shape[0] * groups))
    return (renewed[None], hidden, input_grad, scaled[None])


def solution(mesh):
    in_specs = (P("dp", None), P("dp", "shard", None), P("dp", "shard"), P(), P())
    out_specs = (
        P("dp", "shard", None),
        P("dp", "shard"),
        P(("dp", "shard"), None),
        P("dp", "shard", None),
    )
    return jax.shard_map(body, mesh=mesh, in_specs=in_specs, out_specs=out_specs, check_vma=False)
```

profile of v0, /device:TPU:2, one launch (start us, length us, event | category | flops | bytes accessed | tf_op | source)
XLA Modules:
  0.0 437.4 jit_solution(6716737909057615179)
XLA Ops:
  7.2 0.9 dynamic-slice_reduce_fusion
  8.1 0.3 fusion.28
  8.4 2.1 convolution_bitcast_fusion
  10.5 0.0 copy-start.1
  10.5 1.5 copy.13
  12.0 10.1 %all-to-all-start = ((f32[32,1,5120]{2,1,0:T(1,128)}), f32[32,1,5120]{2,1,0:T(1,128)S(1)}, u32[]{:S(2)}, u32[]{:S(2)}) async-start(f32[32,1,5120]{2,1,0:T(1,128)} %copy.13), calls=%async_computation | async-start | bytes 1310720 | tf_op jit(solution)/shard_map/all_to_all | solution.py:26
  22.1 0.0 all-gather.3.cloned.1.call-start
  22.2 19.8 %all-to-all-done = f32[32,1,5120]{2,1,0:T(1,128)S(1)} async-done(((f32[32,1,5120]{2,1,0:T(1,128)}), f32[32,1,5120]{2,1,0:T(1,128)S(1)}, u32[]{:S(2)}, u32[]{:S(2)}) %all-to-all-start) | async-done | bytes 655392 | tf_op jit(solution)/shard_map/all_to_all | solution.py:26
  41.9 0.0 copy-done.1
  41.9 1.3 convolution_add_fusion.1
  43.2 0.9 convert_bitcast_fusion
  44.1 0.0 all-gather.3.cloned.1.call-update
  44.1 0.2 reduce-scatter.4.cloned.1.call-start
  44.3 76.5 %all-gather.3.cloned.1.call-done = bf16[8,50,5120]{2,1,0:T(8,128)(2,1)} async-done(((bf16[1,50,5120]{2,1,0:T(8,128)(2,1)}), bf16[8,50,5120]{2,1,0:T(8,128)(2,1)}) %all-gather.3.cloned.1.call-update) | async-done | bytes 4096016 | tf_op jit(solution)/shard_map/all_gather | solution.py:29
  120.8 4.3 reshape.14
  125.1 0.0 copy-start
  125.1 0.0 copy-start.2
  125.1 5.6 %fusion.6 = f32[400,1024]{1,0:T(8,128)S(1)} fusion(bf16[1024,2560]{1,0:T(8,128)(2,1)} %param.5, bf16[400,5120]{1,0:T(8,128)(2,1)} %reshape.14), kind=kOutput, calls=%fused_computation.11 | convolution fusion | flops 2097152000 | bytes 8929280 | tf_op jit(solution)/shard_map/td,hd->th/dot_general | solution.py:32
  130.6 0.0 copy-done
  130.6 0.0 copy-done.2
  130.6 6.2 %fusion.10 = (bf16[1024,400]{0,1:T(8,128)(2,1)S(1)}, bf16[1024,400]{0,1:T(8,128)(2,1)}) fusion(bf16[1024,400]{0,1:T(8,128)(2,1)S(1)} %copy-done.2, f32[400,1024]{1,0:T(8,128)S(1)} %fusion.6, bf16[1024,2560]{1,0:T(8,128)(2,1)} %param.5, bf16[400,5120]{1,0:T(8,128)(2,1)S(1)} %copy-done), kind=kOutput, calls=%fused_computation.15 | convolution fusion | flops 2102886400 | bytes 11386880 | tf_op jit(solution)/shard_map/td,hd->th/dot_general | solution.py:33
  136.8 0.0 copy-start.5
  136.8 0.9 copy-done.5
  137.7 2.9 fusion.4
  140.6 6.0 %convolution_add_fusion = f32[1024,2560]{1,0:T(8,128)} fusion(f32[1024,2560]{1,0:T(8,128)S(1)} %fusion.4, bf16[400,5120]{1,0:T(8,128)(2,1)S(1)} %copy-done, bf16[1024,400]{0,1:T(8,128)(2,1)S(1)} %copy-done.2, f32[400,1024]{1,0:T(8,128)S(1)} %fusion.6), kind=kOutput, calls=%fused_computation.1 | convolution fusion | flops 2102640640 | bytes 25477120 | tf_op jit(solution)/shard_map/dot_general | solution.py:42
  146.6 0.0 reduce-scatter.4.cloned.1.call-update
  146.6 0.0 copy-start.3
  146.6 5.1 %fusion.29 = f32[400,2560]{1,0:T(8,128)S(1)} fusion(bf16[1024,400]{0,1:T(8,128)(2,1)} %copy-done.5, bf16[1024,2560]{1,0:T(8,128)(2,1)} %param.5), kind=kOutput, calls=%fused_computation.44 | convolution fusion | flops 2097152000 | bytes 10158080 | tf_op jit(solution)/shard_map/th,td->hd/dot_general | solution.py:50
  151.7 0.0 copy-done.3
  151.7 4.9 %fusion.25 = f32[400,2560]{1,0:T(8,128)S(1)} fusion(bf16[1024,2560]{1,0:T(8,128)(2,1)} %param.5, bf16[1024,400]{0,1:T(8,128)(2,1)S(1)} %copy-done.3, f32[400,1024]{1,0:T(8,128)S(1)} %fusion.6), kind=kOutput, calls=%fused_computation.42 | convolution fusion | flops 2100019200 | bytes 11796480 | tf_op jit(solution)/shard_map/th,td->hd/dot_general | solution.py:51
  156.6 4.0 pad_maximum_fusion
  160.6 233.4 %fusion = f32[56,5120]{1,0:T(8,128)S(1)} fusion(f32[400,5120]{1,0:T(8,128)} %pad_maximum_fusion), kind=kCustom, calls=%all-reduce-scatter | all-reduce-scatter fusion | flops 2293761 | bytes 9339904
  394.0 0.0 copy-start.4
  394.0 1.0 slice.10
  395.1 2.3 collective-permute-start
  397.3 0.0 copy-done.4
  397.3 0.6 dynamic-slice.4
  398.6 2.0 copy.14
  400.6 18.0 %collective-permute-done = f32[42,5120]{1,0:T(8,128)S(1)} collective-permute-done((f32[42,5120]{1,0:T(8,128)}, f32[42,5120]{1,0:T(8,128)S(1)}, u32[]{:S(2)}, u32[]{:S(2)}) %collective-permute-start) | collective-permute-done | bytes 860192
  418.6 6.8 %concatenate.4 = f32[98,5120]{1,0:T(8,128)} concatenate(f32[42,5120]{1,0:T(8,128)S(1)} %collective-permute-done, f32[56,5120]{1,0:T(8,128)S(1)} %fusion), dimensions={0} | concatenate | bytes 4014080
  425.5 1.4 fusion.17
  426.9 2.0 copy.15
  428.9 0.0 reduce-scatter.4.cloned.1.call-done
  428.9 1.7 convert_element_type.25
  (1 shorter events, 0.0 us)
Async XLA Ops:
  10.5 31.4 %copy-start.1 = (f32[1,50,5120]{2,0,1:T(1,128)S(1)}, f32[1,50,5120]{2,0,1:T(1,128)}, u32[]{:S(2)}) copy-start(f32[1,50,5120]{2,0,1:T(1,128)} %param.6) | copy-start | bytes 3072004
  12.0 29.9 %all-to-all-start = ((f32[32,1,5120]{2,1,0:T(1,128)}), f32[32,1,5120]{2,1,0:T(1,128)S(1)}, u32[]{:S(2)}, u32[]{:S(2)}) async-start(f32[32,1,5120]{2,1,0:T(1,128)} %copy.13), calls=%async_computation | async-start | bytes 1310720 | tf_op jit(solution)/shard_map/all_to_all | solution.py:26
  22.1 98.7 %all-gather.3.cloned.1.call-start = ((), (), s32[]{:S(2)}) async-start(), calls=%async_computation.3 | async-start | bytes 5160960 | tf_op jit(solution)/shard_map/all_gather | solution.py:29
  44.1 384.8 %reduce-scatter.4.cloned.1.call-start = ((), (), s32[]{:S(2)}) async-start(), calls=%async_computation.2 | async-start | bytes 10813440 | tf_op jit(solution)/shard_map/reduce_scatter | solution.py:40
  125.1 5.6 %copy-start = (bf16[400,5120]{1,0:T(8,128)(2,1)S(1)}, bf16[400,5120]{1,0:T(8,128)(2,1)}, u32[]{:S(2)}) copy-start(bf16[400,5120]{1,0:T(8,128)(2,1)} %reshape.14) | copy-start | bytes 12288004
  125.1 5.6 %copy-start.2 = (bf16[1024,400]{0,1:T(8,128)(2,1)S(1)}, bf16[1024,400]{0,1:T(8,128)(2,1)}, u32[]{:S(2)}) copy-start(bf16[1024,400]{0,1:T(8,128)(2,1)} %param.7) | copy-start | bytes 2457604
  136.8 0.9 copy-start.5
  146.6 5.1 %copy-start.3 = (bf16[1024,400]{0,1:T(8,128)(2,1)S(1)}, bf16[1024,400]{0,1:T(8,128)(2,1)}, u32[]{:S(2)}) copy-start(bf16[1024,400]{0,1:T(8,128)(2,1)} %param.7) | copy-start | bytes 2457604
  394.0 3.3 copy-start.4
  395.1 23.6 %collective-permute-start = (f32[42,5120]{1,0:T(8,128)}, f32[42,5120]{1,0:T(8,128)S(1)}, u32[]{:S(2)}, u32[]{:S(2)}) collective-permute-start(f32[42,5120]{1,0:T(8,128)} %slice.10), channel_id=1, source_target_pairs={{0,32},{32,64},{64,96},{96,128},{128,160},{160,192},{192,224},{1,3... | collective-permute-start | bytes 2580488
Sparse Core Ops, SparseCore 0:
  44.2 76.5 all-gather.2
  146.8 133.5 reduce-scatter.3
where the time goes:
time: 441 us; the launch traced here: 437 us
  blocking collectives  233 us (53%)
  waiting for transfers between devices  114 us (26%)
  matrix products  34.2 us (8%)
  local copies, waits for them, and re-layouts  20.1 us (5%)
  between operations  14.8 us (3%)
  starting transfers between devices  12.6 us (3%)
  other arithmetic  7.93 us (2%)
    unnamed x1, blocking collectives  233 us
    all_gather x1, waiting for transfers between devices, body(): lax.all_gather(renewed.astype(jnp.bfloat16), 'dp', axis=0, tiled=True)  76.5 us
    all_to_all x1, waiting for transfers between devices, body(): lax.all_to_all(outgoing, 'shard', split_axis=0, concat_axis=0, tiled=True)  19.8 us
    unnamed x3, waiting for transfers between devices  18.1 us
    unnamed x18, local copies, waits for them, and re-layouts  17.7 us
    all_to_all x1, starting transfers between devices, body(): lax.all_to_all(outgoing, 'shard', split_axis=0, concat_axis=0, tiled=True)  10.1 us
  transfers between devices with their start and end apart: 4, of which 3 were waited for; matrix products, arithmetic and copies ran while one was open for 60% of the time, Pallas kernels for 0%

commit v1 on v0

v1 whole, which is shorter than its diff:
```python
import functools
import math

import jax
import jax.numpy as jnp
from jax import lax
from jax.experimental import pallas as pl
from jax.experimental.pallas import tpu as pltpu
from jax.sharding import PartitionSpec as P

MESH = pl.DeviceIdType.MESH
F32, BF16 = jnp.float32, jnp.bfloat16

NY, NXH, NXL, NZ, NC = 4, 2, 2, 8, 2
SHARDS = NXL * NZ * NC
PAGES = 50
D = 2560
TOK = 1024
HALF = D // 2
QUART = D // 4
MAIN = 48
TILE = 16
PAY = 4 * MAIN + TILE
UP0 = 128
ROWS = TOK // 2


def permutation_matrix(shape, page_dim):
    col = lax.broadcasted_iota(jnp.int32, shape, page_dim)
    pos = lax.broadcasted_iota(jnp.int32, shape, 1 - page_dim)
    group = pos // 128
    lane = pos - group * 128
    inside = jnp.where(
        lane < MAIN,
        lane,
        jnp.where(lane < 2 * MAIN, lane + 2, jnp.where(lane < 98, lane - 48, lane)),
    )
    source = jnp.where(lane < 100, group * 100 + inside, -1)
    return jnp.where(col == source, 1.0, 0.0).astype(BF16)


def kernel(
    idx, masters, tokens_hbm, cot_hbm,
    out_masters, out_hidden, out_ig, out_grads,
    tok, cot, cotp, hid, outgoing, incoming, xs, xr, w, dbuf, dt, dwb, dwown,
    ra, rb, rc, fin, xs2, xr2, ig, igs, igr, zs, zr, ls, lr,
    psend, precv, ssem, rsem, lsem,
):
    dp = lax.axis_index("dp")
    me = lax.axis_index("shard")
    y, xh = dp // 2, dp % 2
    xl, z, core = me // 16, (me // 2) % 8, me % 2
    yr, yl, yo = (y + 1) % NY, (y + NY - 1) % NY, (y + 2) % NY
    right_y = (yr * 2 + xh, me)
    left_y = (yl * 2 + xh, me)
    xpartner = (y * 2 + 1 - xh, me)
    cpartner = (dp, me + 1 - 2 * core)
    lpartner = (dp, (1 - xl) * 16 + z * 2 + core)
    right_z = (dp, xl * 16 + ((z + 1) % NZ) * 2 + core)
    left_z = (dp, xl * 16 + ((z + NZ - 1) % NZ) * 2 + core)
    ydir = (right_y, left_y)
    zdir = (right_z, left_z)

    count = [0]

    def remote(src, dst, device):
        n = count[0]
        count[0] += 1
        return pltpu.make_async_remote_copy(
            src_ref=src, dst_ref=dst, send_sem=ssem.at[n], recv_sem=rsem.at[n],
            device_id=device, device_id_type=MESH,
        )

    started = []

    def start(copy):
        copy.start()
        started.append(copy)
        return copy

    load_tok = pltpu.make_async_copy(tokens_hbm, tok, lsem.at[0])
    load_cot = pltpu.make_async_copy(cot_hbm, cot, lsem.at[1])
    load_cot.start()
    load_tok.start()

    barrier = pltpu.get_barrier_semaphore()
    for peer in (right_y, left_y, xpartner):
        pl.semaphore_signal(barrier, inc=1, device_id=peer, device_id_type=MESH)

    def greet(k, carry):
        pl.semaphore_signal(
            barrier, inc=1, device_id=(dp, (me + k) % SHARDS), device_id_type=MESH
        )
        return carry

    lax.fori_loop(1, SHARDS, greet, 0)
    incoming[me] = jnp.zeros((1, 2 * D), F32)
    pl.semaphore_wait(barrier, 3 + SHARDS - 1)

    def page_copy(t):
        return pltpu.make_async_remote_copy(
            src_ref=outgoing.at[t], dst_ref=incoming.at[me],
            send_sem=psend.at[t], recv_sem=precv.at[me],
            device_id=(dp, t), device_id_type=MESH,
        )

    def page_out(k, carry):
        t = (me + k) % SHARDS
        outgoing[t] = masters[pl.ds(idx[t], 1), :]
        page_copy(t).start()
        return carry

    lax.fori_loop(1, SHARDS, page_out, 0)

    for g in range(NY):
        w[g, 112:128, :] = jnp.zeros((16, D), BF16)
        w[g, 240:256, :] = jnp.zeros((16, D), BF16)
    load_cot.wait()
    for r in range(4):
        rows = pl.ds(r * 256, 256)
        moved = jnp.dot(
            cot[rows, :], permutation_matrix((8 * PAGES, NY * 128), 0), preferred_element_type=F32
        ).astype(BF16)
        for g in range(NY):
            cotp[g, rows, :] = moved[:, g * 128 : (g + 1) * 128]
    load_tok.wait()

    def page_wait(k, carry):
        t = (me + k) % SHARDS
        pltpu.make_async_remote_copy(
            src_ref=outgoing.at[t], dst_ref=incoming.at[t],
            send_sem=psend.at[t], recv_sem=precv.at[t],
            device_id=(dp, t), device_id_type=MESH,
        ).wait()
        return carry

    lax.fori_loop(1, SHARDS, page_wait, 0)

    for j in range(PAGES):
        p = idx[SHARDS + j]
        out_masters[j : j + 1, :] = jnp.where(
            p < 0, masters[j : j + 1, :], incoming[jnp.maximum(p, 0)]
        )

    gate_at = pl.multiple_of(MAIN * xh, 16)
    gate_ot = pl.multiple_of(MAIN * (1 - xh), 16)
    up_at = pl.multiple_of(UP0 + MAIN * xh, 16)
    up_ot = pl.multiple_of(UP0 + MAIN * (1 - xh), 16)
    none = jnp.zeros((6, D), F32)
    xs[0:MAIN, :] = out_masters[0:MAIN, 0:D].astype(BF16)
    xs[MAIN : 2 * MAIN, :] = out_masters[0:MAIN, D:].astype(BF16)
    last = out_masters[MAIN:PAGES, :]
    xs[2 * MAIN :, :] = jnp.concatenate([last[:, 0:D], none, last[:, D:], none], axis=0).astype(BF16)
    xcopy = start(remote(xs, xr, xpartner))
    w[y, pl.ds(gate_at, MAIN), :] = xs[0:MAIN, :]
    w[y, pl.ds(up_at, MAIN), :] = xs[MAIN : 2 * MAIN, :]

    def wslice(g, at, size):
        return w.at[g, pl.ds(at, size), :]

    spans = ((gate_at, MAIN), (up_at, MAIN), (gate_ot, MAIN), (up_ot, MAIN), (96, TILE))
    direct = {}

    def send_span(p):
        for dirn in range(2):
            ref = wslice(y, *spans[p])
            direct[dirn, p] = start(remote(ref, ref, ydir[dirn]))

    send_span(0)
    send_span(1)
    xcopy.wait_recv()
    w[y, pl.ds(gate_ot, MAIN), :] = xr[0:MAIN, :]
    w[y, pl.ds(up_ot, MAIN), :] = xr[MAIN : 2 * MAIN, :]
    mine = xs[2 * MAIN :, :].astype(F32)
    theirs = xr[2 * MAIN :, :].astype(F32)
    first = jnp.where(xh == 0, mine, theirs)
    second = jnp.where(xh == 0, theirs, mine)
    none4 = jnp.zeros((4, D), F32)
    w[y, 96:112, :] = jnp.concatenate(
        [first[0:2], second[0:2], none4, first[8:10], second[8:10], none4], axis=0
    ).astype(BF16)
    send_span(2)
    send_span(3)
    send_span(4)

    def place_tile(g):
        t = w[g, 96:112, :].astype(F32)
        w[g, 224:240, :] = jnp.concatenate([t[8:16], t[0:8]], axis=0).astype(BF16)

    def forward_group(g, begin):
        @pl.loop(0, 2)
        def _(step):
            r = (step + 1 - xl) % 2
            rows = pl.ds(pl.multiple_of(r * ROWS, ROWS), ROWS)
            both = lax.dot_general(
                tok[rows, :], w[g], (((1,), (1,)), ((), ())), preferred_element_type=F32
            )
            gate, up = both[:, 0:128], both[:, 128:256]
            grad_in = cotp[g, rows, :].astype(F32)
            sig = jax.nn.sigmoid(gate)
            active = gate * sig
            hid[g, rows, :] = (active * up).astype(BF16)
            d_gate = (grad_in * up * sig * (1.0 + gate * (1.0 - sig))).astype(BF16)
            d_up = (grad_in * active).astype(BF16)
            dbuf[rows, 0:128] = d_gate
            dbuf[rows, 128:256] = d_up
            dt[0:128, rows] = d_gate.T
            dt[128:256, rows] = d_up.T
            at = pl.ds(pl.multiple_of(r * 8, 8), 8)
            for n in range(5):
                cols = pl.ds(n * 512, 512)
                term = jnp.dot(dbuf[rows, :], w[g, :, cols], preferred_element_type=F32)
                term = term.reshape(8, 2, 32, 512)
                if begin:
                    ig[at, :, :, cols] = term
                else:
                    ig[at, :, :, cols] = ig[at, :, :, cols] + term

    def page_grads(h):
        cols = pl.ds(h * HALF, HALF)
        return jnp.dot(dt[...], tok[:, cols], preferred_element_type=F32)

    def put_grads(dst, h, kind):
        cols = pl.ds(h * HALF, HALF)
        part = page_grads(h)
        dst[0:96, cols] = part[0:96].astype(kind)
        dst[96:112, cols] = jnp.concatenate([part[96:104], part[224:232]], axis=0).astype(kind)
        dst[112:208, cols] = part[128:224].astype(kind)

    place_tile(y)
    forward_group(y, True)
    put_grads(dwown, 0, F32)
    put_grads(dwown, 1, F32)

    onward = {}
    for p, dirn in ((0, 0), (1, 1), (2, 0), (3, 1), (4, 0)):
        direct[dirn, p].wait_recv()
        g = (yl, yr)[dirn]
        ref = wslice(g, *spans[p])
        onward[p] = start(remote(ref, ref, ydir[dirn]))

    early = []
    for dirn in (0, 1):
        for p in range(5):
            if (p, dirn) not in ((0, 0), (1, 1), (2, 0), (3, 1), (4, 0)):
                direct[dirn, p].wait_recv()
        g = (yl, yr)[dirn]
        slot = (1, 0)[dirn]
        place_tile(g)
        forward_group(g, False)
        put_grads(dwb.at[slot], 0, BF16)
        put_grads(dwb.at[slot], 1, BF16)
        to, h = (1, 0) if dirn == 0 else (0, 1)
        early.append((to, start(remote(dwb.at[slot, :, pl.ds(h * HALF, HALF)], ra.at[to], ydir[to]))))
    early = dict(early)

    for p in range(5):
        onward[p].wait_recv()
    place_tile(yo)
    forward_group(yo, False)

    corec = {}
    for k in range(2):
        c = (1 - xl, xl)[k]
        at = pl.ds(pl.multiple_of(c * 8, 8), 8)

        @pl.loop(0, 8)
        def _(i):
            igs[c * 8 + i] = ig[c * 8 + i, 1 - core].astype(BF16)

        corec[k] = start(remote(igs.at[at], igr.at[at], cpartner))

    far = {}
    for h in range(2):
        put_grads(dwb.at[2], h, BF16)
        for q in range(2):
            cols = pl.ds(h * HALF + q * QUART, QUART)
            far[h, q] = start(remote(dwb.at[2, :, cols], rb.at[h, q], ydir[h]))

    zc = {}

    def z_step(step, k):
        c = (1 - xl, xl)[k]
        if step == 1:
            corec[k].wait_recv()
        for dirn in range(2):
            owner = (z + (5 - step)) % NZ if dirn == 0 else (z + NZ - (5 - step)) % NZ
            at = c * 8 + owner
            if step == 1:
                cols = pl.ds(dirn * HALF, HALF)
                zs[dirn, 0, k, :, cols] = (
                    ig[at, core, :, cols] + igr[at, :, cols].astype(F32)
                ).astype(BF16)
                zc[1, k, dirn] = start(
                    remote(zs.at[dirn, 0, k, :, cols], zr.at[dirn, 0, k, :, cols], zdir[dirn])
                )
                continue
            zc[step - 1, k, dirn].wait_recv()
            for h in range(2):
                cols = pl.ds(h * HALF, HALF)
                term = ig[at, core, :, cols] + igr[at, :, cols].astype(F32)
                if step > 2 or h == dirn:
                    term = term + zr[dirn, step - 2, k, :, cols].astype(F32)
                zs[dirn, step - 1, k, :, cols] = term.astype(BF16)
            zc[step, k, dirn] = start(
                remote(zs.at[dirn, step - 1, k], zr.at[dirn, step - 1, k], zdir[dirn])
            )

    second_hop = {}

    def pass_on(q):
        for dirn in range(2):
            far[dirn, q].wait_recv()
            cols = pl.ds(dirn * HALF + q * QUART, QUART)
            dwb[dirn, :, cols] = (
                dwb[dirn, :, cols].astype(F32) + rb[dirn, q].astype(F32)
            ).astype(BF16)
            second_hop[dirn, q] = start(remote(dwb.at[dirn, :, cols], rc.at[dirn, q], ydir[dirn]))

    xc = {}

    def collect(q):
        for h in range(2):
            second_hop[h, q].wait_recv()
            if q == 0:
                early[1 - h].wait_recv()
            cols = pl.ds(h * HALF + q * QUART, QUART)
            here = pl.ds(q * QUART, QUART)

            def total(rows):
                return (
                    dwown[rows, cols]
                    + rc[h, q, rows, :].astype(F32)
                    + ra[1 - h, rows, here].astype(F32)
                )

            def rows_of(at, size):
                return pl.ds(pl.multiple_of(at, 16), size)

            xs2[h, q, 0:MAIN, :] = total(rows_of(MAIN * (1 - xh), MAIN)).astype(BF16)
            xs2[h, q, MAIN : 2 * MAIN, :] = total(rows_of(112 + MAIN * (1 - xh), MAIN)).astype(BF16)
            shared = total(pl.ds(96, TILE))
            xs2[h, q, 2 * MAIN :, :] = shared.astype(BF16)
            xc[h, q] = start(remote(xs2.at[h, q], xr2.at[h, q], xpartner))
            fin[0:MAIN, cols] = total(rows_of(MAIN * xh, MAIN))
            fin[MAIN : 2 * MAIN, cols] = total(rows_of(112 + MAIN * xh, MAIN))
            fin[2 * MAIN :, cols] = shared

    def finish(q):
        scale = 1.0 / math.sqrt(TOK * NY * NXH)
        for h in range(2):
            xc[h, q].wait_recv()
            cols = pl.ds(h * HALF + q * QUART, QUART)
            ucols = pl.ds(D + h * HALF + q * QUART, QUART)
            whole = (fin[:, cols] + xr2[h, q].astype(F32)) * scale
            out_grads[0:MAIN, cols] = whole[0:MAIN]
            out_grads[0:MAIN, ucols] = whole[MAIN : 2 * MAIN]
            t = whole[2 * MAIN :]
            out_grads[MAIN:PAGES, cols] = jnp.where(xh == 0, t[0:2], t[2:4])
            out_grads[MAIN:PAGES, ucols] = jnp.where(xh == 0, t[8:10], t[10:12])

    def z_total(k):
        c = (1 - xl, xl)[k]
        at = c * 8 + z
        for dirn in range(2):
            zc[4, k, dirn].wait_recv()
        return (
            ig[at, core]
            + igr[at].astype(F32)
            + zr[0, 3, k].astype(F32)
            + zr[1, 3, k].astype(F32)
        )

    z_step(1, 0)
    z_step(1, 1)
    z_step(2, 0)
    z_step(2, 1)
    for r in range(4):
        rows = pl.ds(r * 256, 256)
        flat = jnp.concatenate([hid[g, rows, :] for g in range(NY)], axis=1)
        out_hidden[rows, :] = jnp.dot(
            flat, permutation_matrix((NY * 128, 8 * PAGES), 1), preferred_element_type=F32
        ).astype(BF16)
    pass_on(0)
    z_step(3, 0)
    z_step(3, 1)
    pass_on(1)
    z_step(4, 0)
    z_step(4, 1)
    collect(0)
    ls[...] = z_total(0).astype(BF16)
    lcopy = start(remote(ls, lr, lpartner))
    collect(1)
    finish(0)
    own = z_total(1)
    lcopy.wait_recv()
    out_ig[...] = (own + lr[...].astype(F32)).astype(BF16)
    finish(1)
    for copy in started:
        copy.wait_send()


def body(tokens, masters, cotangent, partner, slots):
    member = lax.axis_index("shard")
    my_partner = lax.dynamic_index_in_dim(partner, member, 1, False)
    my_slot = lax.dynamic_index_in_dim(slots, member, 1, False)
    peers = jnp.arange(SHARDS, dtype=jnp.int32)
    pages = jnp.arange(PAGES, dtype=jnp.int32)
    give = jnp.sum(jnp.where(my_partner[:, None] == peers[None, :], my_slot[:, None], 0), axis=0)
    take = jnp.sum(jnp.where(my_slot[:, None] == pages[None, :], my_partner[:, None] + 1, 0), axis=0) - 1
    idx = jnp.concatenate([give, take])
    vmem = pl.BlockSpec(memory_space=pltpu.VMEM)
    n_remote = 64
    outs = pl.pallas_call(
        kernel,
        out_shape=(
            jax.ShapeDtypeStruct((PAGES, 2 * D), F32),
            jax.ShapeDtypeStruct((TOK, 8 * PAGES), BF16),
            jax.ShapeDtypeStruct((32, D), BF16),
            jax.ShapeDtypeStruct((PAGES, 2 * D), F32),
        ),
        in_specs=[
            pl.BlockSpec(memory_space=pltpu.SMEM),
            vmem,
            pl.BlockSpec(memory_space=pl.ANY),
            pl.BlockSpec(memory_space=pl.ANY),
        ],
        out_specs=(vmem,) * 4,
        scratch_shapes=[
            pltpu.VMEM((TOK, D), BF16),
            pltpu.VMEM((TOK, 8 * PAGES), BF16),
            pltpu.VMEM((NY, TOK, 128), BF16),
            pltpu.VMEM((NY, TOK, 128), BF16),
            pltpu.VMEM((SHARDS, 1, 2 * D), F32),
            pltpu.VMEM((SHARDS, 1, 2 * D), F32),
            pltpu.VMEM((112, D), BF16),
            pltpu.VMEM((112, D), BF16),
            pltpu.VMEM((NY, 256, D), BF16),
            pltpu.VMEM((TOK, 256), BF16),
            pltpu.VMEM((256, TOK), BF16),
            pltpu.VMEM((3, PAY, D), BF16),
            pltpu.VMEM((PAY, D), F32),
            pltpu.VMEM((2, PAY, HALF), BF16),
            pltpu.VMEM((2, 2, PAY, QUART), BF16),
            pltpu.VMEM((2, 2, PAY, QUART), BF16),
            pltpu.VMEM((112, D), F32),
            pltpu.VMEM((2, 2, 112, QUART), BF16),
            pltpu.VMEM((2, 2, 112, QUART), BF16),
            pltpu.VMEM((16, 2, 32, D), F32),
            pltpu.VMEM((16, 32, D), BF16),
            pltpu.VMEM((16, 32, D), BF16),
            pltpu.VMEM((2, 4, 2, 32, D), BF16),
            pltpu.VMEM((2, 4, 2, 32, D), BF16),
            pltpu.VMEM((32, D), BF16),
            pltpu.VMEM((32, D), BF16),
            pltpu.SemaphoreType.DMA((SHARDS,)),
            pltpu.SemaphoreType.DMA((SHARDS,)),
            pltpu.SemaphoreType.DMA((n_remote,)),
            pltpu.SemaphoreType.DMA((n_remote,)),
            pltpu.SemaphoreType.DMA((2,)),
        ],
        compiler_params=pltpu.CompilerParams(
            collective_id=0, has_side_effects=True, vmem_limit_bytes=60 * 2**20
        ),
    )(idx, masters[0], tokens, cotangent)
    new, hidden, input_grad, grads = outs
    return (new[None], hidden, input_grad, grads[None])


def solution(mesh):
    in_specs = (P("dp", None), P("dp", "shard", None), P("dp", "shard"), P(), P())
    out_specs = (
        P("dp", "shard", None),
        P("dp", "shard"),
        P(("dp", "shard"), None),
        P("dp", "shard", None),
    )
    return jax.shard_map(body, mesh=mesh, in_specs=in_specs, out_specs=out_specs, check_vma=False)
```

time: 441 us -> 140 us (0.32)
  blocking collectives: 233 us -> 0 us
  Pallas kernels: 0 us -> 126 us
  waiting for transfers between devices: 114 us -> 0 us
  matrix products: 34.2 us -> 0 us
  between operations: 14.8 us -> 0.67 us
  starting transfers between devices: 12.6 us -> 0 us
  local copies, waits for them, and re-layouts: 20.1 us -> 10.9 us
  other arithmetic: 7.93 us -> 1.83 us
    unnamed x1 -> x0, blocking collectives: 233 us -> none
    pallas_call x0 -> x1, Pallas kernels: none -> 126 us  [body(): pl.pallas_call(kernel, out_shape=(jax.ShapeDtypeStruct((PAGES, 2 * D), F3...]
    all_gather x1 -> x0, waiting for transfers between devices: 76.5 us -> none  [body(): lax.all_gather(renewed.astype(jnp.bfloat16), 'dp', axis=0, tiled=True)]
    dot_general x9 -> x0, matrix products: 34.2 us -> none  [the longest x1 6.15 us: body(): jnp.einsum('td,hd->th', tokens, up_w, preferred_element_type=jnp.float32)]
    all_to_all x1 -> x0, waiting for transfers between devices: 19.8 us -> none  [body(): lax.all_to_all(outgoing, 'shard', split_axis=0, concat_axis=0, tiled=True)]
    unnamed x3 -> x0, waiting for transfers between devices: 18.1 us -> none
    all_to_all x1 -> x0, starting transfers between devices: 10.1 us -> none  [body(): lax.all_to_all(outgoing, 'shard', split_axis=0, concat_axis=0, tiled=True)]
    unnamed x18 -> x14, local copies, waits for them, and re-layouts: 17.7 us -> 10.9 us
  transfers between devices with their start and end apart: 4 -> 0, of which waited for: 3 -> 0; matrix products, arithmetic and copies ran while one was open for 60% -> 0% of each run, Pallas kernels for 0% -> 0%
where the time goes in v1:
time: 140 us
  Pallas kernels  126 us (90%)
  local copies, waits for them, and re-layouts  10.9 us (8%)
  other arithmetic  1.83 us (1%)
    pallas_call x1, Pallas kernels, body(): pl.pallas_call(kernel, out_shape=(jax.ShapeDtypeStruct((PAGES, 2 * D), F3...  126 us
    unnamed x14, local copies, waits for them, and re-layouts  10.9 us

profile of v1, /device:TPU:2, one launch (start us, length us, event | category | flops | bytes accessed | tf_op | source)
XLA Modules:
  0.0 139.8 jit_solution(17455316889152215082)
XLA Ops:
  0.6 0.0 copy-start.2
  0.6 1.0 dynamic-slice_reduce_fusion.1
  1.7 0.1 select_reduce_fusion.1
  1.8 0.1 select_reduce_fusion
  1.9 0.6 pad_add_fusion.idx
  2.5 2.2 %copy.17.cot_hbm = bf16[1024,400]{1,0:T(8,128)(2,1)} copy(bf16[1024,400]{0,1:T(8,128)(2,1)} %param.7) | data formatting | bytes 1638400 | tf_op args[2]
  4.7 0.0 copy-done.2
  4.7 1.2 copy.23
  5.9 126.4 %shard_map.84 = (f32[50,5120]{1,0:T(8,128)}, bf16[1024,400]{1,0:T(8,128)(2,1)}, bf16[32,2560]{1,0:T(8,128)(2,1)}, f32[50,5120]{1,0:T(8,128)}) custom-call(s32[82]{0:T(128)} %pad_add_fusion.idx, f32[50,5120]{1,0:T(8,128)} %bitcast.5, bf16[1024,2560]{1,0:T(8,128)(2,1)} %tokens_hbm.1, bf16[1024,400]{1,0:T(8,128)(2,1)} %copy.17.cot_hbm), custom_call_target="tpu_custom_call" | custom-call | tf_op jit(solution)/shard_map/pallas_call | solution.py:414
  132.3 0.0 copy-start.1
  132.3 3.4 %copy.18 = f32[1,50,5120]{2,0,1:T(1,128)} copy(f32[1,50,5120]{2,1,0:T(8,128)} %bitcast.7) | data formatting | bytes 2048000
  135.7 0.0 copy-done.1
  135.7 0.0 copy-start
  135.7 1.2 copy.19
  136.9 0.2 copy-done
  137.1 0.0 copy-start.3
  137.1 2.0 %copy.20 = f32[1,50,5120]{2,0,1:T(1,128)} copy(f32[1,50,5120]{2,1,0:T(8,128)S(1)} %bitcast.6) | data formatting | bytes 2048000
  139.1 0.0 copy-done.3
  139.1 0.7 copy.25
  (1 shorter events, 0.0 us)
Async XLA Ops:
  0.6 4.1 %copy-start.2 = (f32[1,50,5120]{2,0,1:T(1,128)S(1)}, f32[1,50,5120]{2,0,1:T(1,128)}, u32[]{:S(2)}) copy-start(f32[1,50,5120]{2,0,1:T(1,128)} %param.6) | copy-start | bytes 3072004
  132.3 3.4 %copy-start.1 = (bf16[1024,400]{1,0:T(8,128)(2,1)S(1)}, bf16[1024,400]{1,0:T(8,128)(2,1)}, u32[]{:S(2)}) copy-start(bf16[1024,400]{1,0:T(8,128)(2,1)} %get-tuple-element.21) | copy-start | bytes 2457604
  135.7 1.4 %copy-start = (f32[50,5120]{1,0:T(8,128)S(1)}, f32[50,5120]{1,0:T(8,128)}, u32[]{:S(2)}) copy-start(f32[50,5120]{1,0:T(8,128)} %get-tuple-element.11) | copy-start | bytes 3072004
  137.1 2.0 %copy-start.3 = (bf16[32,2560]{1,0:T(8,128)(2,1)S(1)}, bf16[32,2560]{1,0:T(8,128)(2,1)}, u32[]{:S(2)}) copy-start(bf16[32,2560]{1,0:T(8,128)(2,1)} %get-tuple-element.33) | copy-start | bytes 491524

commit v2 on v1

v2 whole, which is shorter than its diff:
```python
import functools
import math

import jax
import jax.numpy as jnp
from jax import lax
from jax.experimental import pallas as pl
from jax.experimental.pallas import tpu as pltpu
from jax.sharding import PartitionSpec as P

MESH = pl.DeviceIdType.MESH
F32, BF16 = jnp.float32, jnp.bfloat16

NY, NXH, NXL, NZ, NC = 4, 2, 2, 8, 2
SHARDS = NXL * NZ * NC
MOVED = SHARDS - 1
PAGES = 50
KEPT = PAGES - MOVED
UNITS = NY * NXH * PAGES
D = 2560
TOK = 1024
HALF = D // 2
PIECES = 5
WIDE = HALF // PIECES
CROSS = 2
EARLY = 16
MAIN = 48
TILE = 16
PAY = 4 * MAIN + TILE
UP0 = 128
ROWS = TOK // 2
LANES = NY * 128
N_SENDS = 128


def prepare(partner, slots, idx, source):
    me = lax.axis_index("shard")

    def clear(j, carry):
        idx[SHARDS + j] = -1
        return carry

    lax.fori_loop(0, PAGES, clear, 0, unroll=True)

    def note(r, carry):
        p, s = partner[r, me], slots[r, me]
        idx[p] = s
        idx[SHARDS + s] = p
        return carry

    lax.fori_loop(0, MOVED, note, 0, unroll=True)
    lane = lax.broadcasted_iota(jnp.int32, (1, LANES), 1)
    group = lane // 128
    lane = lane - group * 128
    place = jnp.where(
        lane < 2 * MAIN, lane % MAIN, jnp.where(lane < 100, MAIN + lane % 2, -1)
    )
    block = jnp.where(lane < 2 * MAIN, lane // MAIN, (lane - 2 * MAIN) // 2)

    def put(j, carry):
        count, unit = carry
        p = idx[SHARDS + j]
        kept = p < 0
        at = jnp.where(kept, count, KEPT + (p + SHARDS - me - 1) % SHARDS)
        idx[SHARDS + PAGES + at] = j
        idx[SHARDS + 2 * PAGES + j] = at
        unit = jnp.where(place == at, j, unit)
        return count + jnp.where(kept, 1, 0), unit

    _, unit = lax.fori_loop(0, PAGES, put, (0, jnp.zeros((1, LANES), jnp.int32)), unroll=True)
    source[...] = jnp.where(place < 0, -1, group * (2 * PAGES) + block * PAGES + unit)


def kernel(
    idx, source, masters, tokens_hbm, cot_hbm,
    out_masters, out_hidden, out_ig, out_grads,
    tok, cot, cotp, hid, outgoing, incoming, stage, tx, tr, w, wo, d, do, dt, dwb, dwown,
    ra, rx, sb, rb, rc, fin, xs2, xr2, ig, zs, zr, ls, lr,
    psend, precv, ssem, rsem, lsem,
):
    dp = lax.axis_index("dp")
    me = lax.axis_index("shard")
    y, xh = dp // 2, dp % 2
    xl, z, core = me // 16, (me // 2) % 8, me % 2
    yr, yl, yo = (y + 1) % NY, (y + NY - 1) % NY, (y + 2) % NY
    right_y = (yr * 2 + xh, me)
    left_y = (yl * 2 + xh, me)
    xpartner = (y * 2 + 1 - xh, me)
    cpartner = (dp, me + 1 - 2 * core)
    lpartner = (dp, (1 - xl) * 16 + z * 2 + core)
    right_z = (dp, xl * 16 + ((z + 1) % NZ) * 2 + core)
    left_z = (dp, xl * 16 + ((z + NZ - 1) % NZ) * 2 + core)
    ydir = (right_y, left_y)
    zdir = (right_z, left_z)

    count = [0]
    started = []

    def send(src, dst, device):
        n = count[0]
        count[0] += 1
        copy = pltpu.make_async_remote_copy(
            src_ref=src, dst_ref=dst, send_sem=ssem.at[n], recv_sem=rsem.at[n],
            device_id=device, device_id_type=MESH,
        )
        copy.start()
        started.append(copy)
        return copy

    load_tok = pltpu.make_async_copy(tokens_hbm, tok, lsem.at[0])
    load_cot = pltpu.make_async_copy(cot_hbm, cot, lsem.at[1])
    load_cot.start()
    load_tok.start()

    barrier = pltpu.get_barrier_semaphore()
    for peer in (right_y, left_y, xpartner):
        pl.semaphore_signal(barrier, inc=1, device_id=peer, device_id_type=MESH)

    def greet(k, carry):
        pl.semaphore_signal(
            barrier, inc=1, device_id=(dp, (me + k) % SHARDS), device_id_type=MESH
        )
        return carry

    lax.fori_loop(1, SHARDS, greet, 0)
    incoming[me] = jnp.zeros((1, 2 * D), F32)

    def page_fill(k, carry):
        t = (me + k) % SHARDS
        outgoing[t] = masters[idx[t]]
        return carry

    lax.fori_loop(1, SHARDS, page_fill, 0)

    def at(kind, b, part):
        return pl.multiple_of(kind * UP0 + MAIN * b + (0, EARLY)[part], 16)

    size = (EARLY, MAIN - EARLY)

    def span(g, kind, b, part):
        return w.at[g, pl.ds(at(kind, b, part), size[part]), :]

    def put_block(part):
        begin = (0, EARLY)[part]
        for kind in range(2):
            w[y, pl.ds(at(kind, xh, part), size[part]), :] = stage[
                begin : begin + size[part], kind * D : (kind + 1) * D
            ].astype(BF16)

    for i in range(EARLY):
        stage[i : i + 1, :] = masters[idx[SHARDS + PAGES + i]]
    put_block(0)

    pl.semaphore_wait(barrier, 3 + SHARDS - 1)

    def page_out(k, carry):
        t = (me + k) % SHARDS
        pltpu.make_async_remote_copy(
            src_ref=outgoing.at[t], dst_ref=incoming.at[me],
            send_sem=psend.at[t], recv_sem=precv.at[me],
            device_id=(dp, t), device_id_type=MESH,
        ).start()
        return carry

    other = 1 - xh
    xa, own, ot, fwd, x2 = {}, {}, {}, {}, {}

    def spread(table, kind, b, part):
        for dirn in range(2):
            ref = span(y, kind, b, part)
            table[kind, part, dirn] = send(ref, ref, ydir[dirn])

    def give_x(part):
        for kind in range(2):
            ref = span(y, kind, xh, part)
            xa[kind, part] = send(ref, ref, xpartner)

    def take_x(part):
        for kind in range(2):
            xa[kind, part].wait_recv()
            spread(ot, kind, other, part)

    def forward_on(part):
        for kind in range(2):
            own[kind, part, kind].wait_recv()
            ref = span((yl, yr)[kind], kind, xh, part)
            fwd[kind, part] = send(ref, ref, ydir[kind])

    def cross(part):
        for kind in range(2):
            fwd[kind, part].wait_recv()
            ref = span(yo, kind, xh, part)
            x2[kind, part] = send(ref, ref, xpartner)

    lax.fori_loop(1, SHARDS, page_out, 0)
    give_x(0)
    for kind in range(2):
        spread(own, kind, xh, 0)
    for g in range(NY):
        for ref in (w, wo):
            ref[g, 112:128, :] = jnp.zeros((16, D), BF16)
            ref[g, 240:256, :] = jnp.zeros((16, D), BF16)

    def matrix():
        unit = lax.broadcasted_iota(jnp.int32, (UNITS, LANES), 0)
        return jnp.where(unit == source[...], 1.0, 0.0).astype(BF16)

    take_x(0)
    load_cot.wait()
    for r in range(2):
        rows = pl.ds(r * ROWS, ROWS)
        moved = lax.dot_general(
            cot[:, rows], matrix(), (((0,), (0,)), ((), ())), preferred_element_type=F32
        ).astype(BF16)
        for g in range(NY):
            cotp[g, rows, :] = moved[:, g * 128 : (g + 1) * 128]
    forward_on(0)
    load_tok.wait()
    cross(0)

    for i in range(EARLY, KEPT):
        stage[i : i + 1, :] = masters[idx[SHARDS + PAGES + i]]

    def page_wait(k, carry):
        t = (me + k) % SHARDS
        pltpu.make_async_remote_copy(
            src_ref=outgoing.at[t], dst_ref=incoming.at[t],
            send_sem=psend.at[t], recv_sem=precv.at[t],
            device_id=(dp, t), device_id_type=MESH,
        ).wait()
        return carry

    lax.fori_loop(1, SHARDS, page_wait, 0)
    for k in range(MOVED):
        stage[KEPT + k : KEPT + k + 1, :] = incoming[(me + 1 + k) % SHARDS]
    put_block(1)
    give_x(1)
    none = jnp.zeros((6, D), F32)
    last = stage[MAIN:PAGES, :]
    tx[...] = jnp.concatenate([last[:, 0:D], none, last[:, D:], none], axis=0).astype(BF16)
    tcopy = send(tx, tr, xpartner)
    for kind in range(2):
        spread(own, kind, xh, 1)

    for j in range(PAGES):
        p = idx[SHARDS + j]
        out_masters[j] = jnp.where(p < 0, masters[j], incoming[jnp.maximum(p, 0)])

    forward_on(1)
    take_x(1)
    tcopy.wait_recv()
    mine, theirs = tx[...].astype(F32), tr[...].astype(F32)
    first = jnp.where(xh == 0, mine, theirs)
    second = jnp.where(xh == 0, theirs, mine)
    none4 = jnp.zeros((4, D), F32)
    w[y, 96:112, :] = jnp.concatenate(
        [first[0:2], second[0:2], none4, first[8:10], second[8:10], none4], axis=0
    ).astype(BF16)
    shared = {}
    for dirn in range(2):
        ref = w.at[y, 96:112, :]
        shared[dirn] = send(ref, ref, ydir[dirn])

    def place_tile(ref):
        t = ref[96:112, :].astype(F32)
        ref[224:240, :] = jnp.concatenate([t[8:16], t[0:8]], axis=0).astype(BF16)

    cw, cd = {}, {}

    def share_group(name, g):
        place_tile(w.at[g])
        cw[name] = [
            send(w.at[g, rows, :], wo.at[g, rows, :], cpartner)
            for rows in (pl.ds(0, 112), pl.ds(UP0, 96))
        ]

    def forward_group(name, g):
        @pl.loop(0, 2)
        def _(r):
            rows = pl.ds(pl.multiple_of(r * ROWS, ROWS), ROWS)
            both = lax.dot_general(
                tok[rows, :], w[g], (((1,), (1,)), ((), ())), preferred_element_type=F32
            )
            gate, up = both[:, 0:128], both[:, 128:256]
            grad_in = cotp[g, rows, :].astype(F32)
            sig = jax.nn.sigmoid(gate)
            active = gate * sig
            hid[rows, pl.ds(pl.multiple_of(g * 128, 128), 128)] = (active * up).astype(BF16)
            d_gate = (grad_in * up * sig * (1.0 + gate * (1.0 - sig))).astype(BF16)
            d_up = (grad_in * active).astype(BF16)
            half = pl.ds(pl.multiple_of(r * 8, 8), 8)
            for k, part in ((0, d_gate), (1, d_up)):
                part4 = part.reshape(8, 2, 32, 128)
                for c in range(2):
                    d[g, c, half, :, k * 128 : (k + 1) * 128] = part4[:, c]
                dt[name, k * 128 : (k + 1) * 128, rows] = part.T

        cd[name] = send(d.at[g, 1 - core], do.at[g], cpartner)

    def token_terms(groups, begin):
        @pl.loop(0, 2)
        def _(step):
            r = (step + 1 - xl) % 2
            half = pl.ds(pl.multiple_of(r * 8, 8), 8)
            for n in range(5):
                cols = pl.ds(n * 512, 512)
                terms = [] if begin else [ig[half, :, cols].reshape(256, 512)]
                for g in groups:
                    for left, right in ((d.at[g, core], w.at[g]), (do.at[g], wo.at[g])):
                        terms.append(
                            jnp.dot(
                                left[half].reshape(256, 256), right[:, cols],
                                preferred_element_type=F32,
                            )
                        )
                ig[half, :, cols] = functools.reduce(jnp.add, terms).reshape(8, 32, 512)

    def put_grads(name, dst, h, kind):
        cols = pl.ds(h * HALF, HALF)
        part = jnp.dot(dt[name], tok[:, cols], preferred_element_type=F32)
        dst[0:96, cols] = part[0:96].astype(kind)
        dst[96:112, cols] = jnp.concatenate([part[96:104], part[224:232]], axis=0).astype(kind)
        dst[112:208, cols] = part[128:224].astype(kind)

    def core_wait(name, g):
        for copy in cw[name]:
            copy.wait_recv()
        place_tile(wo.at[g])
        cd[name].wait_recv()

    RIGHT, LEFT, FAR, OWN = range(4)
    share_group(OWN, y)
    forward_group(OWN, y)
    cross(1)
    shared[0].wait_recv()
    ref = w.at[yl, 96:112, :]
    onward = send(ref, ref, right_y)
    put_grads(OWN, dwown, 0, F32)
    put_grads(OWN, dwown, 1, F32)
    core_wait(OWN, y)
    token_terms((y,), True)

    early = {}
    for dirn, name, g in ((0, LEFT, yl), (1, RIGHT, yr)):
        for kind in range(2):
            for part in range(2):
                ot[kind, part, dirn].wait_recv()
                if kind != dirn:
                    own[kind, part, dirn].wait_recv()
        if dirn == 1:
            shared[1].wait_recv()
        share_group(name, g)
        forward_group(name, g)
        to, h = (1, 0) if dirn == 0 else (0, 1)
        put_grads(name, dwb.at[name], h, BF16)
        early[to] = send(dwb.at[name, :, pl.ds(h * HALF, HALF)], ra.at[to], ydir[to])

    for kind in range(2):
        for part in range(2):
            x2[kind, part].wait_recv()
    onward.wait_recv()
    share_group(FAR, yo)
    forward_group(FAR, yo)
    core_wait(LEFT, yl)
    core_wait(RIGHT, yr)
    core_wait(FAR, yo)
    token_terms((yl, yr, yo), False)

    zc = {}

    def z_step(step, k):
        c = (1 - xl, xl)[k]
        for dirn in range(2):
            owner = (z + (5 - step)) % NZ if dirn == 0 else (z + NZ - (5 - step)) % NZ
            row = c * 8 + owner
            if step == 1:
                cols = pl.ds(dirn * HALF, HALF)
                zs[dirn, 0, k, :, cols] = ig[row, :, cols].astype(BF16)
                zc[1, k, dirn] = send(
                    zs.at[dirn, 0, k, :, cols], zr.at[dirn, 0, k, :, cols], zdir[dirn]
                )
                continue
            zc[step - 1, k, dirn].wait_recv()
            for h in range(2):
                cols = pl.ds(h * HALF, HALF)
                term = ig[row, :, cols]
                if step > 2 or h == dirn:
                    term = term + zr[dirn, step - 2, k, :, cols].astype(F32)
                zs[dirn, step - 1, k, :, cols] = term.astype(BF16)
            zc[step, k, dirn] = send(zs.at[dirn, step - 1, k], zr.at[dirn, step - 1, k], zdir[dirn])

    z_step(1, 0)
    z_step(1, 1)

    gate_own = pl.ds(pl.multiple_of(MAIN * xh, 16), MAIN)
    gate_ot = pl.ds(pl.multiple_of(MAIN * other, 16), MAIN)
    up_own = pl.ds(pl.multiple_of(112 + MAIN * xh, 16), MAIN)
    up_ot = pl.ds(pl.multiple_of(112 + MAIN * other, 16), MAIN)
    tile = pl.ds(96, TILE)

    def columns(h, q):
        return pl.ds(h * HALF + q * WIDE, WIDE)

    across, far, second_hop, xc = {}, {}, {}, {}
    for h in range(2):
        put_grads(FAR, dwb.at[FAR], h, BF16)
        for q in range(CROSS):
            across[h, q] = [
                send(dwb.at[FAR, gate_ot, columns(h, q)], rx.at[h, q, 0:MAIN, :], xpartner),
                send(dwb.at[FAR, up_ot, columns(h, q)], rx.at[h, q, MAIN : 2 * MAIN, :], xpartner),
            ]
        for q in range(CROSS, PIECES):
            far[h, q] = send(dwb.at[FAR, :, columns(h, q)], rb.at[h, q], ydir[h])
    put_grads(LEFT, dwb.at[LEFT], 1, BF16)
    put_grads(RIGHT, dwb.at[RIGHT], 0, BF16)

    def join(q):
        for h in range(2):
            for copy in across[h, q]:
                copy.wait_recv()
            cols = columns(h, q)
            for rows, begin in ((gate_own, 0), (up_own, MAIN)):
                sb[h, q, begin : begin + MAIN, :] = (
                    dwb[FAR, rows, cols].astype(F32) + rx[h, q, begin : begin + MAIN, :].astype(F32)
                ).astype(BF16)
            sb[h, q, 2 * MAIN :, :] = dwb[FAR, tile, cols]
            far[h, q] = send(sb.at[h, q], rb.at[h, q, 0:112, :], ydir[h])

    def pass_on(q):
        for h in range(2):
            far[h, q].wait_recv()
            cols = columns(h, q)
            if q < CROSS:
                parts = ((gate_own, 0, MAIN), (up_own, MAIN, MAIN), (tile, 2 * MAIN, TILE))
            else:
                parts = ((pl.ds(0, PAY), 0, PAY),)
            for rows, begin, n in parts:
                dwb[h, rows, cols] = (
                    dwb[h, rows, cols].astype(F32) + rb[h, q, begin : begin + n, :].astype(F32)
                ).astype(BF16)
            second_hop[h, q] = send(dwb.at[h, :, cols], rc.at[h, q], ydir[h])

    def collect(q):
        for h in range(2):
            second_hop[h, q].wait_recv()
            if q == CROSS:
                early[1 - h].wait_recv()
            cols = columns(h, q)
            here = pl.ds(q * WIDE, WIDE)

            def total(rows):
                return (
                    dwown[rows, cols]
                    + rc[h, q, rows, :].astype(F32)
                    + ra[1 - h, rows, here].astype(F32)
                )

            xs2[h, q, 0:MAIN, :] = total(gate_ot).astype(BF16)
            xs2[h, q, MAIN : 2 * MAIN, :] = total(up_ot).astype(BF16)
            both = total(tile)
            xs2[h, q, 2 * MAIN :, :] = both.astype(BF16)
            xc[h, q] = send(xs2.at[h, q], xr2.at[h, q], xpartner)
            fin[0:MAIN, cols] = total(gate_own)
            fin[MAIN : 2 * MAIN, cols] = total(up_own)
            fin[2 * MAIN :, cols] = both

    def finish(q):
        scale = 1.0 / math.sqrt(TOK * NY * NXH)
        for h in range(2):
            xc[h, q].wait_recv()
            cols = columns(h, q)
            ucols = pl.ds(D + h * HALF + q * WIDE, WIDE)
            fin[:, cols] = (fin[:, cols] + xr2[h, q].astype(F32)) * scale
            for j in range(PAGES):
                p = idx[SHARDS + 2 * PAGES + j]
                rest = 2 * MAIN + 2 * xh + p - MAIN
                row = jnp.where(p < MAIN, p, rest)
                urow = jnp.where(p < MAIN, MAIN + p, rest + 8)
                out_grads[j, :, cols] = fin[pl.ds(row, 1), cols]
                out_grads[j, :, ucols] = fin[pl.ds(urow, 1), cols]

    def z_total(k):
        row = (1 - xl, xl)[k] * 8 + z
        for dirn in range(2):
            zc[4, k, dirn].wait_recv()
        return ig[row] + zr[0, 3, k].astype(F32) + zr[1, 3, k].astype(F32)

    z_step(2, 0)
    join(0)
    pass_on(2)
    z_step(2, 1)
    join(1)
    pass_on(3)
    z_step(3, 0)
    pass_on(4)
    pass_on(0)
    z_step(3, 1)
    pass_on(1)
    collect(2)
    z_step(4, 0)
    collect(3)
    z_step(4, 1)
    for r in range(2):
        rows = pl.ds(r * ROWS, ROWS)
        out_hidden[:, rows] = lax.dot_general(
            matrix(), hid[rows, :], (((1,), (1,)), ((), ())), preferred_element_type=F32
        ).astype(BF16)
    collect(4)
    ls[...] = z_total(0).astype(BF16)
    lcopy = send(ls, lr, lpartner)
    collect(0)
    finish(2)
    collect(1)
    finish(3)
    finish(4)
    own_sum = z_total(1)
    lcopy.wait_recv()
    out_ig[...] = (own_sum + lr[...].astype(F32)).astype(BF16)
    finish(0)
    finish(1)

    for copy in started:
        copy.wait_send()


def hand_over(*refs):
    ins, outs, held, (arrive, leave) = refs[0:4], refs[4:8], refs[8:12], refs[12:14]
    reads = [pltpu.make_async_copy(ins[i], held[i], arrive.at[i]) for i in range(4)]
    writes = [pltpu.make_async_copy(held[i], outs[i], leave.at[i]) for i in range(4)]
    for copy in reads:
        copy.start()
    for read, write in zip(reads, writes):
        read.wait()
        write.start()
    for copy in writes:
        copy.wait()


def body(tokens, masters, cotangent, partner, slots):
    vmem = pl.BlockSpec(memory_space=pltpu.VMEM)
    smem = pl.BlockSpec(memory_space=pltpu.SMEM)
    idx, source = pl.pallas_call(
        prepare,
        out_shape=(
            jax.ShapeDtypeStruct((SHARDS + 3 * PAGES,), jnp.int32),
            jax.ShapeDtypeStruct((1, LANES), jnp.int32),
        ),
        in_specs=[smem, smem],
        out_specs=(smem, vmem),
    )(partner, slots)
    outs = pl.pallas_call(
        kernel,
        out_shape=(
            jax.ShapeDtypeStruct((PAGES, 1, 2 * D), F32),
            jax.ShapeDtypeStruct((UNITS, TOK), BF16),
            jax.ShapeDtypeStruct((32, D), BF16),
            jax.ShapeDtypeStruct((PAGES, 1, 2 * D), F32),
        ),
        in_specs=[
            smem,
            vmem,
            vmem,
            pl.BlockSpec(memory_space=pl.ANY),
            pl.BlockSpec(memory_space=pl.ANY),
        ],
        out_specs=(vmem,) * 4,
        scratch_shapes=[
            pltpu.VMEM((TOK, D), BF16),
            pltpu.VMEM((UNITS, TOK), BF16),
            pltpu.VMEM((NY, TOK, 128), BF16),
            pltpu.VMEM((TOK, LANES), BF16),
            pltpu.VMEM((SHARDS, 1, 2 * D), F32),
            pltpu.VMEM((SHARDS, 1, 2 * D), F32),
            pltpu.VMEM((PAGES + 6, 2 * D), F32),
            pltpu.VMEM((TILE, D), BF16),
            pltpu.VMEM((TILE, D), BF16),
            pltpu.VMEM((NY, 256, D), BF16),
            pltpu.VMEM((NY, 256, D), BF16),
            pltpu.VMEM((NY, 2, 16, 32, 256), BF16),
            pltpu.VMEM((NY, 16, 32, 256), BF16),
            pltpu.VMEM((4, 256, TOK), BF16),
            pltpu.VMEM((3, PAY, D), BF16),
            pltpu.VMEM((PAY, D), F32),
            pltpu.VMEM((2, PAY, HALF), BF16),
            pltpu.VMEM((2, CROSS, 2 * MAIN, WIDE), BF16),
            pltpu.VMEM((2, CROSS, 112, WIDE), BF16),
            pltpu.VMEM((2, PIECES, PAY, WIDE), BF16),
            pltpu.VMEM((2, PIECES, PAY, WIDE), BF16),
            pltpu.VMEM((112, D), F32),
            pltpu.VMEM((2, PIECES, 112, WIDE), BF16),
            pltpu.VMEM((2, PIECES, 112, WIDE), BF16),
            pltpu.VMEM((16, 32, D), F32),
            pltpu.VMEM((2, 4, 2, 32, D), BF16),
            pltpu.VMEM((2, 4, 2, 32, D), BF16),
            pltpu.VMEM((32, D), BF16),
            pltpu.VMEM((32, D), BF16),
            pltpu.SemaphoreType.DMA((SHARDS,)),
            pltpu.SemaphoreType.DMA((SHARDS,)),
            pltpu.SemaphoreType.DMA((N_SENDS,)),
            pltpu.SemaphoreType.DMA((N_SENDS,)),
            pltpu.SemaphoreType.DMA((2,)),
        ],
        compiler_params=pltpu.CompilerParams(
            collective_id=0, has_side_effects=True, vmem_limit_bytes=60 * 2**20
        ),
    )(idx, source, jnp.transpose(masters, (1, 0, 2)), tokens, cotangent.T)
    new, hidden, input_grad, grads = pl.pallas_call(
        hand_over,
        out_shape=tuple(jax.ShapeDtypeStruct(out.shape, out.dtype) for out in outs),
        in_specs=[pl.BlockSpec(memory_space=pl.ANY)] * 4,
        out_specs=(pl.BlockSpec(memory_space=pl.ANY),) * 4,
        scratch_shapes=[pltpu.VMEM(out.shape, out.dtype) for out in outs]
        + [pltpu.SemaphoreType.DMA((4,))] * 2,
    )(*outs)
    return (
        jnp.transpose(new, (1, 0, 2)),
        hidden.T,
        input_grad,
        jnp.transpose(grads, (1, 0, 2)),
    )


def solution(mesh):
    in_specs = (P("dp", None), P("dp", "shard", None), P("dp", "shard"), P(), P())
    out_specs = (
        P("dp", "shard", None),
        P("dp", "shard"),
        P(("dp", "shard"), None),
        P("dp", "shard", None),
    )
    return jax.shard_map(body, mesh=mesh, in_specs=in_specs, out_specs=out_specs, check_vma=False)
```

time: 140 us -> 115 us (0.82)
  Pallas kernels: 126 us -> 113 us
  local copies, waits for them, and re-layouts: 10.9 us -> 0 us
  other arithmetic: 1.83 us -> 0 us
    pallas_call x1 -> x3, Pallas kernels: 126 us -> 113 us  [the longest x1 108 us: body(): pl.pallas_call(kernel, out_shape=(jax.ShapeDtypeStruct((PAGES, 1, 2 * D),...]
    unnamed x14 -> x0, local copies, waits for them, and re-layouts: 10.9 us -> none
where the time goes in v2:
time: 115 us; the launch traced here: 114 us
  Pallas kernels  113 us (98%)
    pallas_call x1, Pallas kernels, body(): pl.pallas_call(kernel, out_shape=(jax.ShapeDtypeStruct((PAGES, 1, 2 * D),...  108 us
    pallas_call x1, Pallas kernels, body(): pl.pallas_call(hand_over, out_shape=tuple((jax.ShapeDtypeStruct(out.shape...  2.91 us
    pallas_call x1, Pallas kernels, body(): pl.pallas_call(prepare, out_shape=(jax.ShapeDtypeStruct((SHARDS + 3 * PAG...  2.47 us

profile of v2, /device:TPU:2, one launch (start us, length us, event | category | flops | bytes accessed | tf_op | source)
XLA Modules:
  0.0 114.2 jit_solution(11747795025699840753)
XLA Ops:
  0.6 2.5 %shard_map.84 = (s32[182]{0:T(256)}, s32[1,512]{1,0:T(1,128)}) custom-call(s32[31,32]{1,0:T(8,128)} %partner.1, s32[31,32]{1,0:T(8,128)} %slots.1), custom_call_target="tpu_custom_call" | custom-call | tf_op jit(solution)/shard_map/pallas_call | solution.py:542
  3.1 108.0 %shard_map.85 = (f32[50,1,5120]{2,1,0:T(1,128)}, bf16[400,1024]{1,0:T(8,128)(2,1)}, bf16[32,2560]{1,0:T(8,128)(2,1)}, f32[50,1,5120]{2,1,0:T(1,128)}) custom-call(s32[182]{0:T(256)} %get-tuple-element.14.idx, s32[1,512]{1,0:T(1,128)} %get-tuple-element.15.source, f32[50,1,5120]{2,1,0:T(1,128)} %bitcast.5, bf16[1024,2560]{1,0:T(8,128)(2,1)} %tokens_hbm.1, ...), custom_call_target="tpu_custom_call" | custom-call | tf_op jit(solution)/shard_map/pallas_call | solution.py:551
  111.2 2.9 %shard_map.86 = (f32[50,1,5120]{2,1,0:T(1,128)}, bf16[400,1024]{1,0:T(8,128)(2,1)}, bf16[32,2560]{1,0:T(8,128)(2,1)}, f32[50,1,5120]{2,1,0:T(1,128)}) custom-call(f32[50,1,5120]{2,1,0:T(1,128)} %get-tuple-element.16.refs_0_, bf16[400,1024]{1,0:T(8,128)(2,1)} %get-tuple-element.17.refs_1_, bf16[32,2560]{1,0:T(8,128)(2,1)} %get-tuple-element.18.refs_2_, ...), custom_call_target="tpu_custom_call" | custom-call | tf_op jit(solution)/shard_map/pallas_call | solution.py:607

commit v3 on v2

--- a/solution.py
+++ b/solution.py
@@ -23,7 +23,8 @@
 PIECES = 5
 WIDE = HALF // PIECES
 CROSS = 2
-EARLY = 16
+PART = 16
+FIRST = 2 * PART - KEPT
 MAIN = 48
 TILE = 16
 PAY = 4 * MAIN + TILE
@@ -33,48 +34,46 @@
 N_SENDS = 128
 
 
-def prepare(partner, slots, idx, source):
-    me = lax.axis_index("shard")
-
-    def clear(j, carry):
-        idx[SHARDS + j] = -1
-        return carry
-
-    lax.fori_loop(0, PAGES, clear, 0, unroll=True)
-
-    def note(r, carry):
-        p, s = partner[r, me], slots[r, me]
-        idx[p] = s
-        idx[SHARDS + s] = p
-        return carry
-
-    lax.fori_loop(0, MOVED, note, 0, unroll=True)
-    lane = lax.broadcasted_iota(jnp.int32, (1, LANES), 1)
+def total(mask, value, axis):
+    return jnp.sum(jnp.where(mask, value, 0), axis=axis, keepdims=True)
+
+
+def plan(me, partner, slots, table, source):
+    def iota(shape, axis):
+        return lax.broadcasted_iota(jnp.int32, shape, axis)
+
+    mine = iota((MOVED, SHARDS), 1) == me
+    peer_c, slot_c = total(mine, partner[...], 1), total(mine, slots[...], 1)
+    sub, lane = iota((MOVED, 128), 0), iota((MOVED, 128), 1)
+    peer_r, slot_r = total(sub == lane, peer_c, 0), total(sub == lane, slot_c, 0)
+    give_r = total(lane == peer_c, slot_c, 0)
+    take_r = total(lane == slot_c, peer_c + 1, 0) - 1
+    sub, lane = iota((64, 128), 0), iota((64, 128), 1)
+    take_c = total((sub == slot_r) & (lane < MOVED), peer_r + 1, 1) - 1
+
+    def place(take, before):
+        ahead = take - me - 1
+        return jnp.where(take < 0, before, KEPT + jnp.where(ahead < 0, ahead + SHARDS, ahead))
+
+    place_r = place(take_r, total((take_c < 0) & (sub < PAGES) & (sub < lane), 1, 0))
+    place_c = place(take_c, total((take_r < 0) & (lane < PAGES) & (lane < sub), 1, 1))
+    order_r = total((place_c == lane) & (sub < PAGES), sub, 0)
+    for i, row in enumerate((give_r, take_r, order_r, place_r)):
+        table[i : i + 1, :] = row
+    lane = iota((1, LANES), 1)
     group = lane // 128
     lane = lane - group * 128
-    place = jnp.where(
-        lane < 2 * MAIN, lane % MAIN, jnp.where(lane < 100, MAIN + lane % 2, -1)
-    )
+    at = jnp.where(lane < 2 * MAIN, lane % MAIN, jnp.where(lane < 100, MAIN + lane % 2, -1))
     block = jnp.where(lane < 2 * MAIN, lane // MAIN, (lane - 2 * MAIN) // 2)
-
-    def put(j, carry):
-        count, unit = carry
-        p = idx[SHARDS + j]
-        kept = p < 0
-        at = jnp.where(kept, count, KEPT + (p + SHARDS - me - 1) % SHARDS)
-        idx[SHARDS + PAGES + at] = j
-        idx[SHARDS + 2 * PAGES + j] = at
-        unit = jnp.where(place == at, j, unit)
-        return count + jnp.where(kept, 1, 0), unit
-
-    _, unit = lax.fori_loop(0, PAGES, put, (0, jnp.zeros((1, LANES), jnp.int32)), unroll=True)
-    source[...] = jnp.where(place < 0, -1, group * (2 * PAGES) + block * PAGES + unit)
+    sub = iota((64, LANES), 0)
+    unit = total((place_c == at) & (sub < PAGES), sub, 0)
+    source[...] = jnp.where(at < 0, -1, group * (2 * PAGES) + block * PAGES + unit)
 
 
 def kernel(
-    idx, source, masters, tokens_hbm, cot_hbm,
+    partner, slots, masters, tokens_hbm, cot_hbm,
     out_masters, out_hidden, out_ig, out_grads,
-    tok, cot, cotp, hid, outgoing, incoming, stage, tx, tr, w, wo, d, do, dt, dwb, dwown,
+    table, idx, source, tok, cot, cotp, hid, outgoing, incoming, stage, tx, tr, w, wo, d, do, dt, dwb, dwown,
     ra, rx, sb, rb, rc, fin, xs2, xr2, ig, zs, zr, ls, lr,
     psend, precv, ssem, rsem, lsem,
 ):
@@ -123,33 +122,34 @@
         return carry
 
     lax.fori_loop(1, SHARDS, greet, 0)
+    plan(me, partner, slots, table, source)
+    load_idx = pltpu.make_async_copy(table, idx, lsem.at[2])
+    load_idx.start()
     incoming[me] = jnp.zeros((1, 2 * D), F32)
+    load_idx.wait()
 
     def page_fill(k, carry):
         t = (me + k) % SHARDS
-        outgoing[t] = masters[idx[t]]
+        outgoing[t] = masters[idx[0, t]]
         return carry
 
     lax.fori_loop(1, SHARDS, page_fill, 0)
 
     def at(kind, b, part):
-        return pl.multiple_of(kind * UP0 + MAIN * b + (0, EARLY)[part], 16)
-
-    size = (EARLY, MAIN - EARLY)
+        return pl.multiple_of(kind * UP0 + MAIN * b + PART * part, 16)
 
     def span(g, kind, b, part):
-        return w.at[g, pl.ds(at(kind, b, part), size[part]), :]
+        return w.at[g, pl.ds(at(kind, b, part), PART), :]
 
     def put_block(part):
-        begin = (0, EARLY)[part]
+        begin = PART * part
         for kind in range(2):
-            w[y, pl.ds(at(kind, xh, part), size[part]), :] = stage[
-                begin : begin + size[part], kind * D : (kind + 1) * D
+            w[y, pl.ds(at(kind, xh, part), PART), :] = stage[
+                begin : begin + PART, kind * D : (kind + 1) * D
             ].astype(BF16)
 
-    for i in range(EARLY):
-        stage[i : i + 1, :] = masters[idx[SHARDS + PAGES + i]]
-    put_block(0)
+    for i in range(PART):
+        stage[i : i + 1, :] = masters[idx[2, i]]
 
     pl.semaphore_wait(barrier, 3 + SHARDS - 1)
 
@@ -192,10 +192,15 @@
             ref = span(yo, kind, xh, part)
             x2[kind, part] = send(ref, ref, xpartner)
 
-    lax.fori_loop(1, SHARDS, page_out, 0)
-    give_x(0)
-    for kind in range(2):
-        spread(own, kind, xh, 0)
+    def own_out(part):
+        put_block(part)
+        give_x(part)
+        for kind in range(2):
+            spread(own, kind, xh, part)
+
+    lax.fori_loop(1, FIRST + 1, page_out, 0)
+    own_out(0)
+    lax.fori_loop(FIRST + 1, SHARDS, page_out, 0)
     for g in range(NY):
         for ref in (w, wo):
             ref[g, 112:128, :] = jnp.zeros((16, D), BF16)
@@ -205,7 +210,24 @@
         unit = lax.broadcasted_iota(jnp.int32, (UNITS, LANES), 0)
         return jnp.where(unit == source[...], 1.0, 0.0).astype(BF16)
 
+    def page_wait(k, carry):
+        t = (me + k) % SHARDS
+        pltpu.make_async_remote_copy(
+            src_ref=outgoing.at[t], dst_ref=incoming.at[t],
+            send_sem=psend.at[t], recv_sem=precv.at[t],
+            device_id=(dp, t), device_id_type=MESH,
+        ).wait()
+        return carry
+
+    def pages_in(begin, end):
+        lax.fori_loop(begin + 1, end + 1, page_wait, 0)
+        for k in range(begin, end):
+            stage[KEPT + k : KEPT + k + 1, :] = incoming[(me + 1 + k) % SHARDS]
+
+    for i in range(PART, KEPT):
+        stage[i : i + 1, :] = masters[idx[2, i]]
     take_x(0)
+    forward_on(0)
     load_cot.wait()
     for r in range(2):
         rows = pl.ds(r * ROWS, ROWS)
@@ -214,40 +236,26 @@
         ).astype(BF16)
         for g in range(NY):
             cotp[g, rows, :] = moved[:, g * 128 : (g + 1) * 128]
-    forward_on(0)
     load_tok.wait()
-    cross(0)
-
-    for i in range(EARLY, KEPT):
-        stage[i : i + 1, :] = masters[idx[SHARDS + PAGES + i]]
-
-    def page_wait(k, carry):
-        t = (me + k) % SHARDS
-        pltpu.make_async_remote_copy(
-            src_ref=outgoing.at[t], dst_ref=incoming.at[t],
-            send_sem=psend.at[t], recv_sem=precv.at[t],
-            device_id=(dp, t), device_id_type=MESH,
-        ).wait()
-        return carry
-
-    lax.fori_loop(1, SHARDS, page_wait, 0)
-    for k in range(MOVED):
-        stage[KEPT + k : KEPT + k + 1, :] = incoming[(me + 1 + k) % SHARDS]
-    put_block(1)
-    give_x(1)
+    pages_in(0, FIRST)
+    own_out(1)
+    take_x(1)
+    forward_on(1)
+    pages_in(FIRST, MOVED)
+    own_out(2)
     none = jnp.zeros((6, D), F32)
     last = stage[MAIN:PAGES, :]
     tx[...] = jnp.concatenate([last[:, 0:D], none, last[:, D:], none], axis=0).astype(BF16)
     tcopy = send(tx, tr, xpartner)
-    for kind in range(2):
-        spread(own, kind, xh, 1)
+    cross(0)
+    cross(1)
 
     for j in range(PAGES):
-        p = idx[SHARDS + j]
+        p = idx[1, j]
         out_masters[j] = jnp.where(p < 0, masters[j], incoming[jnp.maximum(p, 0)])
 
-    forward_on(1)
-    take_x(1)
+    take_x(2)
+    forward_on(2)
     tcopy.wait_recv()
     mine, theirs = tx[...].astype(F32), tr[...].astype(F32)
     first = jnp.where(xh == 0, mine, theirs)
@@ -297,23 +305,22 @@
 
         cd[name] = send(d.at[g, 1 - core], do.at[g], cpartner)
 
-    def token_terms(groups, begin):
-        @pl.loop(0, 2)
-        def _(step):
-            r = (step + 1 - xl) % 2
-            half = pl.ds(pl.multiple_of(r * 8, 8), 8)
-            for n in range(5):
-                cols = pl.ds(n * 512, 512)
-                terms = [] if begin else [ig[half, :, cols].reshape(256, 512)]
-                for g in groups:
-                    for left, right in ((d.at[g, core], w.at[g]), (do.at[g], wo.at[g])):
-                        terms.append(
-                            jnp.dot(
-                                left[half].reshape(256, 256), right[:, cols],
-                                preferred_element_type=F32,
-                            )
+    def token_terms(groups, begin, k):
+        half = pl.ds(pl.multiple_of((1 - xl, xl)[k] * 8, 8), 8)
+
+        @pl.loop(0, 5)
+        def _(n):
+            cols = pl.ds(pl.multiple_of(n * 512, 512), 512)
+            terms = [] if begin else [ig[half, :, cols].reshape(256, 512)]
+            for g in groups:
+                for left, right in ((d.at[g, core], w.at[g]), (do.at[g], wo.at[g])):
+                    terms.append(
+                        jnp.dot(
+                            left[half].reshape(256, 256), right[:, cols],
+                            preferred_element_type=F32,
                         )
-                ig[half, :, cols] = functools.reduce(jnp.add, terms).reshape(8, 32, 512)
+                    )
+            ig[half, :, cols] = functools.reduce(jnp.add, terms).reshape(8, 32, 512)
 
     def put_grads(name, dst, h, kind):
         cols = pl.ds(h * HALF, HALF)
@@ -331,19 +338,15 @@
     RIGHT, LEFT, FAR, OWN = range(4)
     share_group(OWN, y)
     forward_group(OWN, y)
-    cross(1)
+    cross(2)
     shared[0].wait_recv()
     ref = w.at[yl, 96:112, :]
     onward = send(ref, ref, right_y)
-    put_grads(OWN, dwown, 0, F32)
-    put_grads(OWN, dwown, 1, F32)
-    core_wait(OWN, y)
-    token_terms((y,), True)
 
     early = {}
     for dirn, name, g in ((0, LEFT, yl), (1, RIGHT, yr)):
         for kind in range(2):
-            for part in range(2):
+            for part in range(3):
                 ot[kind, part, dirn].wait_recv()
                 if kind != dirn:
                     own[kind, part, dirn].wait_recv()
@@ -356,15 +359,17 @@
         early[to] = send(dwb.at[name, :, pl.ds(h * HALF, HALF)], ra.at[to], ydir[to])
 
     for kind in range(2):
-        for part in range(2):
+        for part in range(3):
             x2[kind, part].wait_recv()
     onward.wait_recv()
     share_group(FAR, yo)
     forward_group(FAR, yo)
+    core_wait(OWN, y)
     core_wait(LEFT, yl)
     core_wait(RIGHT, yr)
+    for k in range(2):
+        token_terms((y, yl, yr), True, k)
     core_wait(FAR, yo)
-    token_terms((yl, yr, yo), False)
 
     zc = {}
 
@@ -389,8 +394,9 @@
                 zs[dirn, step - 1, k, :, cols] = term.astype(BF16)
             zc[step, k, dirn] = send(zs.at[dirn, step - 1, k], zr.at[dirn, step - 1, k], zdir[dirn])
 
-    z_step(1, 0)
-    z_step(1, 1)
+    for k in range(2):
+        token_terms((yo,), False, k)
+        z_step(1, k)
 
     gate_own = pl.ds(pl.multiple_of(MAIN * xh, 16), MAIN)
     gate_ot = pl.ds(pl.multiple_of(MAIN * other, 16), MAIN)
@@ -404,15 +410,18 @@
     across, far, second_hop, xc = {}, {}, {}, {}
     for h in range(2):
         put_grads(FAR, dwb.at[FAR], h, BF16)
-        for q in range(CROSS):
+        for q in range(CROSS, PIECES):
+            far[h, q] = send(dwb.at[FAR, :, columns(h, q)], rb.at[h, q], ydir[h])
+    for q in range(CROSS):
+        for h in range(2):
             across[h, q] = [
                 send(dwb.at[FAR, gate_ot, columns(h, q)], rx.at[h, q, 0:MAIN, :], xpartner),
                 send(dwb.at[FAR, up_ot, columns(h, q)], rx.at[h, q, MAIN : 2 * MAIN, :], xpartner),
             ]
-        for q in range(CROSS, PIECES):
-            far[h, q] = send(dwb.at[FAR, :, columns(h, q)], rb.at[h, q], ydir[h])
     put_grads(LEFT, dwb.at[LEFT], 1, BF16)
     put_grads(RIGHT, dwb.at[RIGHT], 0, BF16)
+    put_grads(OWN, dwown, 0, F32)
+    put_grads(OWN, dwown, 1, F32)
 
     def join(q):
         for h in range(2):
@@ -448,20 +457,20 @@
             cols = columns(h, q)
             here = pl.ds(q * WIDE, WIDE)
 
-            def total(rows):
+            def summed(rows):
                 return (
                     dwown[rows, cols]
                     + rc[h, q, rows, :].astype(F32)
                     + ra[1 - h, rows, here].astype(F32)
                 )
 
-            xs2[h, q, 0:MAIN, :] = total(gate_ot).astype(BF16)
-            xs2[h, q, MAIN : 2 * MAIN, :] = total(up_ot).astype(BF16)
-            both = total(tile)
+            xs2[h, q, 0:MAIN, :] = summed(gate_ot).astype(BF16)
+            xs2[h, q, MAIN : 2 * MAIN, :] = summed(up_ot).astype(BF16)
+            both = summed(tile)
             xs2[h, q, 2 * MAIN :, :] = both.astype(BF16)
             xc[h, q] = send(xs2.at[h, q], xr2.at[h, q], xpartner)
-            fin[0:MAIN, cols] = total(gate_own)
-            fin[MAIN : 2 * MAIN, cols] = total(up_own)
+            fin[0:MAIN, cols] = summed(gate_own)
+            fin[MAIN : 2 * MAIN, cols] = summed(up_own)
             fin[2 * MAIN :, cols] = both
 
     def finish(q):
@@ -472,7 +481,7 @@
             ucols = pl.ds(D + h * HALF + q * WIDE, WIDE)
             fin[:, cols] = (fin[:, cols] + xr2[h, q].astype(F32)) * scale
             for j in range(PAGES):
-                p = idx[SHARDS + 2 * PAGES + j]
+                p = idx[3, j]
                 rest = 2 * MAIN + 2 * xh + p - MAIN
                 row = jnp.where(p < MAIN, p, rest)
                 urow = jnp.where(p < MAIN, MAIN + p, rest + 8)
@@ -486,38 +495,38 @@
         return ig[row] + zr[0, 3, k].astype(F32) + zr[1, 3, k].astype(F32)
 
     z_step(2, 0)
+    z_step(2, 1)
     join(0)
     pass_on(2)
-    z_step(2, 1)
     join(1)
     pass_on(3)
     z_step(3, 0)
+    collect(2)
     pass_on(4)
-    pass_on(0)
-    z_step(3, 1)
-    pass_on(1)
-    collect(2)
-    z_step(4, 0)
-    collect(3)
-    z_step(4, 1)
     for r in range(2):
         rows = pl.ds(r * ROWS, ROWS)
         out_hidden[:, rows] = lax.dot_general(
             matrix(), hid[rows, :], (((1,), (1,)), ((), ())), preferred_element_type=F32
         ).astype(BF16)
+    pass_on(0)
+    z_step(3, 1)
+    pass_on(1)
+    collect(3)
+    finish(2)
+    z_step(4, 0)
     collect(4)
+    finish(3)
+    collect(0)
+    z_step(4, 1)
+    finish(4)
+    collect(1)
+    finish(0)
     ls[...] = z_total(0).astype(BF16)
     lcopy = send(ls, lr, lpartner)
-    collect(0)
-    finish(2)
-    collect(1)
-    finish(3)
-    finish(4)
+    finish(1)
     own_sum = z_total(1)
     lcopy.wait_recv()
     out_ig[...] = (own_sum + lr[...].astype(F32)).astype(BF16)
-    finish(0)
-    finish(1)
 
     for copy in started:
         copy.wait_send()
@@ -538,16 +547,6 @@
 
 def body(tokens, masters, cotangent, partner, slots):
     vmem = pl.BlockSpec(memory_space=pltpu.VMEM)
-    smem = pl.BlockSpec(memory_space=pltpu.SMEM)
-    idx, source = pl.pallas_call(
-        prepare,
-        out_shape=(
-            jax.ShapeDtypeStruct((SHARDS + 3 * PAGES,), jnp.int32),
-            jax.ShapeDtypeStruct((1, LANES), jnp.int32),
-        ),
-        in_specs=[smem, smem],
-        out_specs=(smem, vmem),
-    )(partner, slots)
     outs = pl.pallas_call(
         kernel,
         out_shape=(
@@ -557,7 +556,7 @@
             jax.ShapeDtypeStruct((PAGES, 1, 2 * D), F32),
         ),
         in_specs=[
-            smem,
+            vmem,
             vmem,
             vmem,
             pl.BlockSpec(memory_space=pl.ANY),
@@ -565,6 +564,9 @@
         ],
         out_specs=(vmem,) * 4,
         scratch_shapes=[
+            pltpu.VMEM((8, 128), jnp.int32),
+            pltpu.SMEM((8, 128), jnp.int32),
+            pltpu.VMEM((1, LANES), jnp.int32),
             pltpu.VMEM((TOK, D), BF16),
             pltpu.VMEM((UNITS, TOK), BF16),
             pltpu.VMEM((NY, TOK, 128), BF16),
@@ -598,12 +600,12 @@
             pltpu.SemaphoreType.DMA((SHARDS,)),
             pltpu.SemaphoreType.DMA((N_SENDS,)),
             pltpu.SemaphoreType.DMA((N_SENDS,)),
-            pltpu.SemaphoreType.DMA((2,)),
+            pltpu.SemaphoreType.DMA((3,)),
         ],
         compiler_params=pltpu.CompilerParams(
             collective_id=0, has_side_effects=True, vmem_limit_bytes=60 * 2**20
         ),
-    )(idx, source, jnp.transpose(masters, (1, 0, 2)), tokens, cotangent.T)
+    )(partner, slots, jnp.transpose(masters, (1, 0, 2)), tokens, cotangent.T)
     new, hidden, input_grad, grads = pl.pallas_call(
         hand_over,
         out_shape=tuple(jax.ShapeDtypeStruct(out.shape, out.dtype) for out in outs),

time: 115 us -> 108 us (0.939)
  Pallas kernels: 113 us -> 107 us
    pallas_call x1, Pallas kernels: 108 us -> 104 us  [body(): pl.pallas_call(kernel, out_shape=(jax.ShapeDtypeStruct((PAGES, 1, 2 * D),...]
    pallas_call x1 -> x0, Pallas kernels: 2.47 us -> none  [body(): pl.pallas_call(prepare, out_shape=(jax.ShapeDtypeStruct((SHARDS + 3 * PAG...]
where the time goes in v3:
time: 108 us
  Pallas kernels  107 us (99%)
    pallas_call x1, Pallas kernels, body(): pl.pallas_call(kernel, out_shape=(jax.ShapeDtypeStruct((PAGES, 1, 2 * D),...  104 us
    pallas_call x1, Pallas kernels, body(): pl.pallas_call(hand_over, out_shape=tuple((jax.ShapeDtypeStruct(out.shape...  2.91 us

profile of v3, /device:TPU:2, one launch (start us, length us, event | category | flops | bytes accessed | tf_op | source)
XLA Modules:
  0.0 107.8 jit_solution(14580370358740034321)
XLA Ops:
  0.6 104.1 %shard_map.84 = (f32[50,1,5120]{2,1,0:T(1,128)}, bf16[400,1024]{1,0:T(8,128)(2,1)}, bf16[32,2560]{1,0:T(8,128)(2,1)}, f32[50,1,5120]{2,1,0:T(1,128)}) custom-call(s32[31,32]{1,0:T(8,128)} %partner.1, s32[31,32]{1,0:T(8,128)} %slots.1, f32[50,1,5120]{2,1,0:T(1,128)} %bitcast.5, bf16[1024,2560]{1,0:T(8,128)(2,1)} %tokens_hbm.1, bf16[400,1024]{1,0:T(8,128)(2,1)} %bitcast.6), custom_call_target="tpu_custom_call" | custom-call | tf_op jit(solution)/shard_map/pallas_call | solution.py:550
  104.7 2.9 %shard_map.85 = (f32[50,1,5120]{2,1,0:T(1,128)}, bf16[400,1024]{1,0:T(8,128)(2,1)}, bf16[32,2560]{1,0:T(8,128)(2,1)}, f32[50,1,5120]{2,1,0:T(1,128)}) custom-call(f32[50,1,5120]{2,1,0:T(1,128)} %get-tuple-element.12.refs_0_, bf16[400,1024]{1,0:T(8,128)(2,1)} %get-tuple-element.13.refs_1_, bf16[32,2560]{1,0:T(8,128)(2,1)} %get-tuple-element.14.refs_2_, ...), custom_call_target="tpu_custom_call" | custom-call | tf_op jit(solution)/shard_map/pallas_call | solution.py:609

commit v4 on v3

--- a/solution.py
+++ b/solution.py
@@ -38,6 +38,14 @@
     return jnp.sum(jnp.where(mask, value, 0), axis=axis, keepdims=True)
 
 
+def peer_at(me, k, sign):
+    turn, rest = k // 4, k % 4
+    ahead = (turn % 2) * ((turn + 1) // 2) + (1 - turn % 2) * ((NZ - turn // 2) % NZ)
+    xl, z, core = me // 16, (me // 2) % NZ, me % 2
+    z = (z + sign * ahead + NZ) % NZ
+    return ((xl + rest // 2) % NXL) * 16 + z * 2 + (core + rest % 2) % NC
+
+
 def plan(me, partner, slots, table, source):
     def iota(shape, axis):
         return lax.broadcasted_iota(jnp.int32, shape, axis)
@@ -52,8 +60,11 @@
     take_c = total((sub == slot_r) & (lane < MOVED), peer_r + 1, 1) - 1
 
     def place(take, before):
-        ahead = take - me - 1
-        return jnp.where(take < 0, before, KEPT + jnp.where(ahead < 0, ahead + SHARDS, ahead))
+        ahead = (take // 2) % NZ - (me // 2) % NZ
+        ahead = jnp.where(ahead < 0, ahead + NZ, ahead)
+        turn = jnp.where(ahead == 0, 0, jnp.where(ahead < 5, 2 * ahead - 1, 2 * (NZ - ahead)))
+        side = jnp.where(take // 16 == me // 16, 0, 2) + jnp.where(take % 2 == me % 2, 0, 1)
+        return jnp.where(take < 0, before, KEPT + 4 * turn + side - 1)
 
     place_r = place(take_r, total((take_c < 0) & (sub < PAGES) & (sub < lane), 1, 0))
     place_c = place(take_c, total((take_r < 0) & (lane < PAGES) & (lane < sub), 1, 1))
@@ -129,7 +140,7 @@
     load_idx.wait()
 
     def page_fill(k, carry):
-        t = (me + k) % SHARDS
+        t = peer_at(me, k, -1)
         outgoing[t] = masters[idx[0, t]]
         return carry
 
@@ -154,7 +165,7 @@
     pl.semaphore_wait(barrier, 3 + SHARDS - 1)
 
     def page_out(k, carry):
-        t = (me + k) % SHARDS
+        t = peer_at(me, k, -1)
         pltpu.make_async_remote_copy(
             src_ref=outgoing.at[t], dst_ref=incoming.at[me],
             send_sem=psend.at[t], recv_sem=precv.at[me],
@@ -198,9 +209,8 @@
         for kind in range(2):
             spread(own, kind, xh, part)
 
-    lax.fori_loop(1, FIRST + 1, page_out, 0)
+    lax.fori_loop(1, SHARDS, page_out, 0)
     own_out(0)
-    lax.fori_loop(FIRST + 1, SHARDS, page_out, 0)
     for g in range(NY):
         for ref in (w, wo):
             ref[g, 112:128, :] = jnp.zeros((16, D), BF16)
@@ -211,7 +221,7 @@
         return jnp.where(unit == source[...], 1.0, 0.0).astype(BF16)
 
     def page_wait(k, carry):
-        t = (me + k) % SHARDS
+        t = peer_at(me, k, 1)
         pltpu.make_async_remote_copy(
             src_ref=outgoing.at[t], dst_ref=incoming.at[t],
             send_sem=psend.at[t], recv_sem=precv.at[t],
@@ -222,7 +232,7 @@
     def pages_in(begin, end):
         lax.fori_loop(begin + 1, end + 1, page_wait, 0)
         for k in range(begin, end):
-            stage[KEPT + k : KEPT + k + 1, :] = incoming[(me + 1 + k) % SHARDS]
+            stage[KEPT + k : KEPT + k + 1, :] = incoming[peer_at(me, k + 1, 1)]
 
     for i in range(PART, KEPT):
         stage[i : i + 1, :] = masters[idx[2, i]]

time: 108 us -> 105 us (0.972)
  Pallas kernels: 107 us -> 104 us
    pallas_call x1, Pallas kernels: 104 us -> 101 us  [body(): pl.pallas_call(kernel, out_shape=(jax.ShapeDtypeStruct((PAGES, 1, 2 * D),...]
where the time goes in v4:
time: 105 us
  Pallas kernels  104 us (99%)
    pallas_call x1, Pallas kernels, body(): pl.pallas_call(kernel, out_shape=(jax.ShapeDtypeStruct((PAGES, 1, 2 * D),...  101 us
    pallas_call x1, Pallas kernels, body(): pl.pallas_call(hand_over, out_shape=tuple((jax.ShapeDtypeStruct(out.shape...  2.91 us

profile of v4, /device:TPU:2, one launch (start us, length us, event | category | flops | bytes accessed | tf_op | source)
XLA Modules:
  0.0 104.8 jit_solution(5877070534471460016)
XLA Ops:
  0.6 101.1 %shard_map.84 = (f32[50,1,5120]{2,1,0:T(1,128)}, bf16[400,1024]{1,0:T(8,128)(2,1)}, bf16[32,2560]{1,0:T(8,128)(2,1)}, f32[50,1,5120]{2,1,0:T(1,128)}) custom-call(s32[31,32]{1,0:T(8,128)} %partner.1, s32[31,32]{1,0:T(8,128)} %slots.1, f32[50,1,5120]{2,1,0:T(1,128)} %bitcast.5, bf16[1024,2560]{1,0:T(8,128)(2,1)} %tokens_hbm.1, bf16[400,1024]{1,0:T(8,128)(2,1)} %bitcast.6), custom_call_target="tpu_custom_call" | custom-call | tf_op jit(solution)/shard_map/pallas_call | solution.py:560
  101.7 2.9 %shard_map.85 = (f32[50,1,5120]{2,1,0:T(1,128)}, bf16[400,1024]{1,0:T(8,128)(2,1)}, bf16[32,2560]{1,0:T(8,128)(2,1)}, f32[50,1,5120]{2,1,0:T(1,128)}) custom-call(f32[50,1,5120]{2,1,0:T(1,128)} %get-tuple-element.12.refs_0_, bf16[400,1024]{1,0:T(8,128)(2,1)} %get-tuple-element.13.refs_1_, bf16[32,2560]{1,0:T(8,128)(2,1)} %get-tuple-element.14.refs_2_, ...), custom_call_target="tpu_custom_call" | custom-call | tf_op jit(solution)/shard_map/pallas_call | solution.py:619
